TPU v7x, 128 devices: a whole 4x4x4 slice. The times are simulated.
128 devices in a mesh: row: 32 (over z, x, y_lo), feat: 4 (over y_hi, core).
Axes of the slice: x: 4, y: 4 (y_hi: 2, y_lo: 2; y = y_hi * 2 + y_lo), z: 4, core: 2. Of those that a mesh axis runs over, the one named last changes fastest.
Arguments:
- cells: bfloat16 [6144, 8, 192], P('row', 'feat'), may hold values from -16 to 16
- w_query: bfloat16 [192, 192], replicated, may hold values from -0.25 to 0.25
- w_key: bfloat16 [192, 192], replicated, may hold values from -0.25 to 0.25
- w_value: bfloat16 [192, 192], replicated, may hold values from -0.4375 to 0.4375
- w_out: bfloat16 [192, 192], replicated, may hold values from -0.4375 to 0.4375
- train_flag: int32 [6144], P('row'), may hold values from 0 to 1, as said below
- grad_out: bfloat16 [6144, 8, 192], P('row', 'feat'), may hold values from -6 to 6
Outputs:
- grad_cells: bfloat16 [6144, 8, 192], P('row', 'feat')
- grad_w_query: float32 [192, 192], replicated
- grad_w_key: float32 [192, 192], replicated
- grad_w_value: float32 [192, 192], replicated
- grad_w_out: float32 [192, 192], replicated
Inputs may be any that keep to these rules, and one draw needn't show every extreme that they name: train_flag is 1 on the first rows of the table and 0 on all later rows; at least 3072 rows are training rows and at least one row is a test row.
All inputs are finite; a program needn't handle non-finite values.
Results may differ from a plain program's by a relative error of at most 0.04.
The roundings to bfloat16 on the way count: a program that leaves them out, or rounds other values in their place, can miss the bound.
Values may be sent and summed in bfloat16 or wider, within the bound.
A program may use at most 128 MiB of HBM per device.

v0:
```python
import jax
import jax.numpy as jnp
from jax import lax
from jax.experimental import pallas as pl
from jax.experimental.pallas import tpu as pltpu
from jax.sharding import PartitionSpec as P


HD = 32
SCALE = float(HD) ** -0.5
SCALE_LOG2E = SCALE * 1.4426950408889634
BIAS = -1e30
F32 = jnp.float32
BF = jnp.bfloat16
MESH = pl.DeviceIdType.MESH

E = 192
HALF = 96
ROWS = 192
NQ = 768
NR = 6144
KC = 768
PC = 384
BLOCKS = 8


def dot(a, b):
    return jnp.dot(a, b, preferred_element_type=F32)


def t_dot(a, b):
    return lax.dot_general(a, b, (((0,), (0,)), ((), ())), preferred_element_type=F32)


def place():
    row = lax.axis_index("row")
    feat = lax.axis_index("feat")
    return row // 8, (row // 2) % 4, row % 2, feat // 2, feat % 2


def device(z, x, yl, yh, c):
    return ((z * 4 + x) * 2 + yl, yh * 2 + c)


def iotas(shape):
    return lax.broadcasted_iota(jnp.int32, shape, 0), lax.broadcasted_iota(jnp.int32, shape, 1)


def ones_where(mask):
    return mask.astype(F32).astype(BF)


def shifted(shape, by, most=None):
    i, j = iotas(shape)
    mask = j == i + by
    if most is not None:
        mask = mask & (i < most)
    return ones_where(mask)


def by_feature():
    i, j = iotas((2 * ROWS, 2 * ROWS))
    second = i >= ROWS
    return ones_where(j == jnp.where(second, 2 * (i - ROWS) + 1, 2 * i))


def rcopy(src, dst, send, recv, to):
    return pltpu.make_async_remote_copy(
        src_ref=src, dst_ref=dst, send_sem=send, recv_sem=recv, device_id=to, device_id_type=MESH
    )


def wait_for(ref, sem):
    pltpu.make_async_copy(ref, ref, sem).wait()


def share_kernel(in_ref, weights, pk_ref, cnt_ref, wkv_ref, u_ref, qT_ref, gT_ref, poT_ref, goT_ref, gp_ref, wqg, cs, gs, cf, cb, four, zb, s1, r1, s2, r2, zs, zr, fs, fr, ts, tr, ns, nr, ms, mr):
    z, x, yl, yh, c = place()
    mine = x // 2 == c
    own = jnp.where(mine, 1, 0)
    zp, zo, zn = (z + 1) % 4, (z + 2) % 4, (z + 3) % 4
    up, down, twin = device(zp, x, yl, yh, c), device(zn, x, yl, yh, c), device(z, x, yl, yh, 1 - c)
    far = device(zo, x, yl, yh, c)
    slot = (x % 2) * 2 + yl

    barrier = pltpu.get_barrier_semaphore()

    def greet(to):
        pl.semaphore_signal(barrier, inc=1, device_id=to, device_id_type=MESH)

    for s in range(4):
        @pl.when(jnp.logical_not(jnp.logical_and(mine, slot == s)))
        def _():
            greet(device(z, 2 * c + s // 2, s % 2, yh, x // 2))
    for to in (up, down, twin):
        greet(to)
    greet(far)

    sort = by_feature()
    left, right = shifted((ROWS, 2 * E), 0), shifted((ROWS, 2 * E), E)

    def pack(first, out):
        rows = dot(sort, in_ref[first:first + ROWS].reshape(2 * ROWS, E)).astype(BF)
        for f in range(2):
            r = f * ROWS
            out[f] = (dot(rows[r:r + HALF], left) + dot(rows[r + HALF:r + ROWS], right)).astype(BF)

    flags = jnp.sum(in_ref[2 * ROWS, 0:1, :].astype(F32), axis=1, keepdims=True)
    cf[...] = jnp.broadcast_to(flags, (8, 128))
    pack(0, cs)
    pl.semaphore_wait(barrier, 4 - own + 4)

    my_rows = pl.ds(pl.multiple_of(((z * 4 + x) * 2 + yl) * HALF, HALF), HALF)
    my_slot = pl.ds(pl.multiple_of(slot * HALF, HALF), HALF)

    def first(j):
        to = device(z, 2 * c + j // 2, j % 2, yh, x // 2)
        a = rcopy(cs.at[j // 2], pk_ref.at[my_rows, :], s1.at[j], r1.at[slot], to)
        b = rcopy(gs.at[j // 2], gp_ref.at[my_slot, :], s2.at[j], r2.at[slot], to)
        return a, b

    for j in range(4):
        keep = jnp.logical_and(mine, slot == j)

        @pl.when(keep)
        def _():
            pltpu.make_async_copy(cs.at[j // 2], pk_ref.at[my_rows, :], r1.at[slot]).start()

        @pl.when(jnp.logical_not(keep))
        def _():
            first(j)[0].start()

    def count(j):
        return rcopy(cf, cb.at[slot], ns.at[j], nr.at[slot], device(z, 2 * c + j // 2, j % 2, yh, x // 2))

    for j in range(4):
        keep = jnp.logical_and(mine, slot == j)

        @pl.when(keep)
        def _():
            pltpu.make_async_copy(cf, cb.at[slot], nr.at[slot]).start()

        @pl.when(jnp.logical_not(keep))
        def _():
            count(j).start()

    def rows_of(zz, cc, s):
        return pl.ds(pl.multiple_of((zz * 2 + cc) * PC + s * HALF, HALF), HALF)

    def move(zz, s, send, recv, to):
        r = rows_of(zz, c, s)
        return rcopy(pk_ref.at[r, :], pk_ref.at[r, :], send, recv, to)

    def landed(zz, cc, s, recv):
        wait_for(pk_ref.at[rows_of(zz, cc, s), :], recv)

    sent = []

    def go(copy):
        copy.start()
        sent.append(copy)

    i, j = iotas((E, 128))
    heads = ones_where((i == j + HALF * yl) & (j < HALF))
    wq = dot(weights[0:192, :], heads).astype(BF)
    wk = dot(weights[192:384, :], heads).astype(BF)
    wv = dot(weights[384:576, :], heads).astype(BF)
    wo = t_dot(weights[576:768, :], heads).astype(BF)
    for out, w in ((wkv_ref, jnp.concatenate([wk, wv], 1)), (wqg.at[0], wq), (wqg.at[1], wo)):
        none = jnp.zeros((64, w.shape[1]), BF)
        out[0, 0:192, :] = w
        out[0, 192:256, :] = none
        out[1, 64:256, :] = w
        out[1, 0:64, :] = none
    for n, w in enumerate((wk, wv, wq)):
        u_ref[0, 128 * n:128 * n + 128, :] = t_dot(w, left).astype(BF)
        u_ref[1, 128 * n:128 * n + 128, :] = t_dot(w, right).astype(BF)

    def own_rows(src, w, out, turned):
        turned[...] = src.T
        out[:, 0:PC] = dot(src[:, 0:256], w[0]).astype(BF).T
        out[:, PC:NQ] = dot(src[:, 128:384], w[1]).astype(BF).T

    for i in range(4):
        s, t = i, (i + 2) % 4
        if i < 2:
            landed(z, c, s, r1.at[s])
            landed(z, c, t, r1.at[t])
        go(move(z, s, zs.at[s], zr.at[s], up))
        go(move(z, t, zs.at[4 + t], zr.at[4 + t], down))
        go(move(z, s, ts.at[s], tr.at[s], twin))

    for s in range(4):
        wait_for(cb.at[s], nr.at[s])
    four[0] = cb[0] + cb[1] + cb[2] + cb[3]
    go(rcopy(four.at[0], four.at[1], ms.at[0], mr.at[0], twin))
    pack(ROWS, gs)
    for j in range(4):
        keep = jnp.logical_and(mine, slot == j)

        @pl.when(keep)
        def _():
            pltpu.make_async_copy(gs.at[j // 2], gp_ref.at[my_slot, :], r2.at[slot]).start()

        @pl.when(jnp.logical_not(keep))
        def _():
            first(j)[1].start()

    own_rows(pk_ref[pl.ds(pl.multiple_of((z * 2 + c) * PC, PC), PC), :], wqg.at[0], qT_ref, poT_ref)
    wait_for(four.at[1], mr.at[0])
    zb[0] = four[0] + four[1]
    for n, to in ((1, up), (2, far), (3, down)):
        go(rcopy(zb.at[0], zb.at[n], ms.at[n], mr.at[n], to))

    for i in range(4):
        s = i
        landed(zn, c, s, zr.at[s])
        if s < 2:
            go(move(zn, s, fs.at[s], fr.at[s], up))
        go(move(zn, s, ts.at[4 + s], tr.at[4 + s], twin))
        s = (i + 2) % 4
        landed(zp, c, s, zr.at[4 + s])
        if s >= 2:
            go(move(zp, s, fs.at[s], fr.at[s], down))
        go(move(zp, s, ts.at[8 + s], tr.at[8 + s], twin))

    for s in (0, 2, 1, 3):
        landed(zo, c, s, fr.at[s])
        go(move(zo, s, ts.at[12 + s], tr.at[12 + s], twin))

    for n in range(1, 4):
        wait_for(zb.at[n], mr.at[n])
    cnt_ref[...] = zb[0] + zb[1] + zb[2] + zb[3]

    for s in range(4):
        wait_for(gp_ref.at[pl.ds(s * HALF, HALF), :], r2.at[s])
    own_rows(gp_ref[...], wqg.at[1], gT_ref, goT_ref)
    for n, zz in ((0, z), (1, zn), (2, zp), (3, zo)):
        for s in range(4):
            landed(zz, 1 - c, s, tr.at[4 * n + s])
    for copy in sent:
        copy.wait_send()
    for j in range(4):
        @pl.when(jnp.logical_not(jnp.logical_and(mine, slot == j)))
        def _():
            a, b = first(j)
            a.wait_send()
            b.wait_send()
            count(j).wait_send()


def attention_kernel(pk_ref, cnt_ref, wkv_ref, u_ref, qT_ref, gT_ref, poT_ref, goT_ref, g_ref, gq_ref, w_ref, e_ref, mb_ref, kv_ref, qm_ref, gm_ref,
                     qmT_ref, gmT_ref, acc_ref, m_ref, s_ref, dkv_ref, attT_ref, dqT_ref, wacc_ref):
    train = jnp.max(cnt_ref[...]).astype(jnp.int32)
    halves = lax.div(train + PC - 1, PC)
    full, odd = lax.div(halves, 2), lax.rem(halves, 2)
    last = lax.div(halves - 1, 2)

    def rows(n):
        return pl.ds(pl.multiple_of(n * KC, KC), KC)

    def packs(n):
        return pl.ds(pl.multiple_of(n * PC, PC), PC)

    def half_packs(n):
        return pl.ds(pl.multiple_of(n * ROWS, ROWS), ROWS)

    @pl.loop(halves, 2 * BLOCKS)
    def _(n):
        g_ref[half_packs(n), :] = jnp.zeros((ROWS, 384), BF)

    lane = lax.broadcasted_iota(jnp.int32, (ROWS, 128), 1)
    sub = lax.broadcasted_iota(jnp.int32, (ROWS, 128), 0)
    real = sub + HALF * (sub >= HALF).astype(jnp.int32)
    v_extra = jnp.where((lane >= HALF) & (lane < HALF + 3), 1.0, 0.0)

    def project(n):
        p = pk_ref[packs(n), :]
        for side, (cells, w) in enumerate(((p[:, 0:256], wkv_ref[0]), (p[:, 128:384], wkv_ref[1]))):
            kv = dot(cells, w)
            for half in range(2):
                first = n * KC + PC * half
                bias = jnp.where((lane == HALF) & (real + (first + HALF * side) >= train), BIAS, 0.0)
                r = pl.ds(pl.multiple_of(first + ROWS * side, ROWS), ROWS)
                own = slice(ROWS * half, ROWS * half + ROWS)
                kv_ref[r, 0:128] = (kv[own, 0:128] + bias).astype(BF)
                kv_ref[r, 128:256] = (kv[own, 128:256] + v_extra).astype(BF)

    project(0)
    project(jnp.minimum(1, last))

    attT_ref[...] = jnp.zeros_like(attT_ref)
    dqT_ref[...] = jnp.zeros_like(dqT_ref)
    wacc_ref[...] = jnp.zeros_like(wacc_ref)
    i16 = lax.broadcasted_iota(jnp.int32, (16, NQ), 0)
    lanes = [slice(NQ * h, NQ * h + NQ) for h in range(3)]
    subs = [slice(32 * h, 32 * h + 32) for h in range(3)]

    qmT_ref[...] = jnp.zeros_like(qmT_ref)
    gmT_ref[...] = jnp.zeros_like(gmT_ref)
    for q, hs in zip(lanes, subs):
        qmT_ref[hs, q] = qT_ref[hs, :]
        qm_ref[q, :] = qmT_ref[:, q].T
        qmT_ref[96:112, q] = jnp.where(i16 == 0, 1.0, 0.0).astype(BF)
    acc_ref[...] = jnp.zeros_like(acc_ref)
    m_ref[...] = jnp.full_like(m_ref, BIAS)

    def piece(n, t):
        return pl.ds(pl.multiple_of(n * KC + (t // 3) * PC, PC), PC), lanes[t % 3]

    def score(n, t):
        r, q = piece(n, t)
        s = dot(kv_ref[r, 0:128], qmT_ref[:, q])
        s_ref[t % 2] = s
        m_ref[2 + t % 2:3 + t % 2, q] = jnp.max(s, axis=0, keepdims=True)

    def weigh(n, t):
        r, q = piece(n, t)
        old = m_ref[0:1, q]
        new = jnp.maximum(old, jnp.ceil(m_ref[2 + t % 2:3 + t % 2, q] * SCALE_LOG2E))
        e = jnp.exp2(s_ref[t % 2] * SCALE_LOG2E - new).astype(BF)
        e_ref[r, q] = e
        m_ref[0:1, q] = new
        mb_ref[n, t // 3:t // 3 + 1, q] = new
        vT = kv_ref[r, 128:256].T
        vt = jnp.concatenate([vT[subs[t % 3]], vT[96:112]], 0)
        acc_ref[:, q] = acc_ref[:, q] * jnp.exp2(old - new) + dot(vt, e)

    score(0, 0)

    @pl.loop(0, full)
    def _(n):
        for t in range(6):
            if t < 5:
                score(n, t + 1)
            else:
                score(jnp.minimum(n + 1, last), 0)
            weigh(n, t)
        project(jnp.minimum(n + 2, last))

    @pl.when(odd == 1)
    def _():
        for t in range(3):
            if t < 2:
                score(full, t + 1)
            weigh(full, t)

    for q, hs in zip(lanes, subs):
        inv = 1.0 / acc_ref[32:33, q]
        att = (acc_ref[0:32, q] * inv).astype(BF)
        attT_ref[hs, :] = att
        gp = (gT_ref[hs, :].astype(F32) * inv).astype(BF)
        delta = -jnp.sum(gp.astype(F32) * att.astype(F32), axis=0, keepdims=True)
        d0 = delta.astype(BF).astype(F32)
        d1 = (delta - d0).astype(BF).astype(F32)
        d2 = delta - d0 - d1
        gmT_ref[hs, q] = gp
        gm_ref[q, :] = gmT_ref[:, q].T
        gmT_ref[96:112, q] = jnp.where(i16 == 0, d0, jnp.where(i16 == 1, d1, jnp.where(i16 == 2, d2, 0.0))).astype(BF)
    acc_ref[...] = jnp.zeros_like(acc_ref)

    def pass_two(n, many):
        size = many * PC
        r = pl.ds(pl.multiple_of(n * KC, KC), size)
        v = kv_ref[r, 128:256]
        kT = kv_ref[r, 0:128].T
        dk, dv = jnp.zeros((size, 128), F32), jnp.zeros((size, 128), F32)
        for h in range(3):
            q = lanes[h]
            ga = dot(v, gmT_ref[:, q]).astype(BF)
            e = e_ref[r, q]
            by = [jnp.exp2(mb_ref[n, t:t + 1, q] - m_ref[0:1, q]).astype(BF) for t in range(many)]
            es = jnp.concatenate([e[PC * t:PC * t + PC] * by[t] for t in range(many)], 0)
            ds = es * ga
            dv = dv + dot(es, gm_ref[q, :])
            dk = dk + dot(ds, qm_ref[q, :])
            acc_ref[0:32, q] += dot(kT[subs[h]], ds)
        dkv_ref[0:size, 0:128] = (dk * SCALE).astype(BF)
        dkv_ref[0:size, 128:256] = dv.astype(BF)
        for t in range(many):
            p = half_packs(2 * n + t)
            pT = pk_ref[p, :].T
            da, db = dkv_ref[PC * t:PC * t + ROWS, :], dkv_ref[PC * t + ROWS:PC * t + PC, :]
            g_ref[p, :] = (dot(da, u_ref[0, 0:256, :]) + dot(db, u_ref[1, 0:256, :])).astype(BF)
            wacc_ref[...] += dot(pT[0:E], da) + dot(pT[E:2 * E], db)

    @pl.loop(0, full)
    def _(n):
        pass_two(n, 2)

    @pl.when(odd == 1)
    def _():
        pass_two(full, 1)

    for q, hs in zip(lanes, subs):
        dqT_ref[hs, :] = (acc_ref[0:32, q] * SCALE).astype(BF)

    dq, at = dqT_ref[...].T, attT_ref[...].T
    gq_ref[...] = dot(dq[0:PC], u_ref[0, 256:384, :]) + dot(dq[PC:NQ], u_ref[1, 256:384, :])
    poT, goT = poT_ref[...], goT_ref[...]
    w_q = dot(poT[0:E], dq[0:PC]) + dot(poT[E:2 * E], dq[PC:NQ])
    w_o = dot(goT[0:E], at[0:PC]) + dot(goT[E:2 * E], at[PC:NQ])
    w_ref[...] = (
        dot(w_q.astype(BF), shifted((128, 384), 0, HALF))
        + dot(w_o.astype(BF), shifted((128, 384), HALF, HALF))
        + dot(wacc_ref[:, 0:128].astype(BF), shifted((128, 384), 2 * HALF, HALF))
        + dot(wacc_ref[:, 128:256].astype(BF), shifted((128, 384), 3 * HALF, HALF))
    ).astype(BF)


def reduce_kernel(g_ref, gq_ref, w_ref, ret_ref, wf_ref,
                  tw, part, hp, hn, fp, fn, fin, rs, p2,
                  ts, tr, hs_, hr, fs, fr, ks, kr, as_, ar, bs, br, cs, cr):
    z, x, yl, yh, c = place()
    mine = x // 2 == c
    own = jnp.where(mine, 1, 0)
    zp, zo, zn = (z + 1) % 4, (z + 2) % 4, (z + 3) % 4
    up, down, twin = device(zp, x, yl, yh, c), device(zn, x, yl, yh, c), device(z, x, yl, yh, 1 - c)
    slot = (x % 2) * 2 + yl
    i16 = z * 4 + x
    i8 = (yh * 2 + yl) * 2 + c
    owner = i16 < SLABS
    owns = jnp.where(owner, 1, 0)

    barrier = pltpu.get_barrier_semaphore()

    def greet(to):
        pl.semaphore_signal(barrier, inc=1, device_id=to, device_id_type=MESH)

    for to in (twin, up, down):
        greet(to)
    for j in range(4):
        @pl.when(jnp.logical_not(jnp.logical_and(mine, slot == j)))
        def _():
            greet(device(z, 2 * c + j // 2, j % 2, yh, x // 2))

    zs_, xs_ = [z, zp, zo, zn], [x, (x + 1) % 4, (x + 2) % 4, (x + 3) % 4]
    around = [(zs_[n // 4], xs_[n % 4]) for n in range(16)]
    beside = [((yl + n // 2 % 2) % 2, (yh + n // 4) % 2, (c + n % 2) % 2) for n in range(8)]
    for n in range(1, 16):
        greet(device(*around[n], yl, yh, c))
    for n in range(1, 8):
        greet(device(z, x, *beside[n]))

    pl.semaphore_wait(barrier, 3 + 4 - own + 15 + 7)

    sent = []

    def go(copy):
        copy.start()
        sent.append(copy)

    def block(zz, cc):
        return pl.ds(pl.multiple_of((zz * 2 + cc) * PC, PC), PC)

    for n, zz in enumerate((zo, zp, zn, z)):
        go(rcopy(g_ref.at[block(zz, 1 - c), :], tw.at[n], ts.at[n], tr.at[n], twin))

    def slab(n):
        return pl.ds(pl.multiple_of(n * 16, 16), 16)

    def one(n):
        zz, xx = around[n]
        to = zz * 4 + xx
        ok = to < SLABS
        r = slab(jnp.minimum(to, SLABS - 1))
        return ok, rcopy(w_ref.at[r, :], rs.at[i16], as_.at[n], ar.at[i16], device(zz, xx, yl, yh, c))

    def two(n):
        return rcopy(p2.at[i8], p2.at[i8], bs.at[n], br.at[i8], device(z, x, *beside[n]))

    my_slab = slab(jnp.minimum(i16, SLABS - 1))

    def three(n):
        mine_ = wf_ref.at[:, my_slab, :]
        return rcopy(mine_, mine_, cs.at[n], cr.at[i16], device(*around[n], yl, yh, c))

    for n in range(1, 16):
        ok, copy = one(n)

        @pl.when(ok)
        def _():
            copy.start()

    def with_twin(n, zz):
        wait_for(tw.at[n], tr.at[n])
        return g_ref[block(zz, c), :].astype(F32) + tw[n].astype(F32)

    lo, hi = pl.ds(0, 192), pl.ds(192, 192)
    part[0] = with_twin(0, zo).astype(BF)
    go(rcopy(part.at[0, lo, :], hp, hs_.at[0], hr.at[0], up))
    go(rcopy(part.at[0, hi, :], hn, hs_.at[1], hr.at[1], down))
    part[1] = with_twin(1, zp).astype(BF)
    go(rcopy(part.at[1, hi, :], fp.at[hi, :], fs.at[0], fr.at[0], up))
    part[2] = with_twin(2, zn).astype(BF)
    go(rcopy(part.at[2, lo, :], fn.at[lo, :], fs.at[1], fr.at[1], down))

    @pl.when(owner)
    def _():
        rs[i16] = w_ref[slab(jnp.minimum(i16, SLABS - 1)), :]

        for n in range(1, 16):
            m = around[n][0] * 4 + around[n][1]
            wait_for(rs.at[m], ar.at[m])

        acc = rs[0].astype(F32)
        for n in range(1, 16):
            acc = acc + rs[n].astype(F32)
        p2[i8] = acc.astype(BF)

        for n in range(1, 8):
            two(n).start()

    wait_for(hp, hr.at[0])
    part[1, 0:192, :] = (part[1, 0:192, :].astype(F32) + hp[...].astype(F32)).astype(BF)
    go(rcopy(part.at[1, lo, :], fp.at[lo, :], fs.at[2], fr.at[2], up))
    wait_for(hn, hr.at[1])
    part[2, 192:384, :] = (part[2, 192:384, :].astype(F32) + hn[...].astype(F32)).astype(BF)
    go(rcopy(part.at[2, hi, :], fn.at[hi, :], fs.at[3], fr.at[3], down))

    @pl.when(owner)
    def _():
        for yl_, yh_, c_ in beside[1:]:
            m = (yh_ * 2 + yl_) * 2 + c_
            wait_for(p2.at[m], br.at[m])

        for half in range(2):
            n = 2 * half
            acc = p2[n].astype(F32) + p2[n + 1].astype(F32) + p2[n + 4].astype(F32) + p2[n + 5].astype(F32)
            wf_ref[half, slab(jnp.minimum(i16, SLABS - 1)), :] = acc.astype(BF)

        for n in range(1, 16):
            three(n).start()

    total = with_twin(3, z) + gq_ref[...]
    wait_for(fp.at[hi, :], fr.at[0])
    wait_for(fn.at[lo, :], fr.at[1])
    wait_for(fp.at[lo, :], fr.at[2])
    wait_for(fn.at[hi, :], fr.at[3])
    fin[...] = (total + fp[...].astype(F32) + fn[...].astype(F32)).astype(BF)

    def back(s):
        to = device(z, 2 * c + s // 2, s % 2, yh, x // 2)
        return rcopy(fin.at[pl.ds(s * HALF, HALF), :], ret_ref.at[slot], ks.at[s], kr.at[slot], to)

    for s in range(4):
        keep = jnp.logical_and(mine, slot == s)

        @pl.when(keep)
        def _():
            pltpu.make_async_copy(fin.at[pl.ds(s * HALF, HALF), :], ret_ref.at[slot], kr.at[slot]).start()

        @pl.when(jnp.logical_not(keep))
        def _():
            back(s).start()

    for n in range(4):
        wait_for(ret_ref.at[n], kr.at[n])

    for n in range(1, 16):
        m = around[n][0] * 4 + around[n][1]

        @pl.when(m < SLABS)
        def _():
            r = slab(jnp.minimum(m, SLABS - 1))
            wait_for(wf_ref.at[:, r, :], cr.at[m])

    for copy in sent:
        copy.wait_send()
    for s in range(4):
        @pl.when(jnp.logical_not(jnp.logical_and(mine, slot == s)))
        def _():
            back(s).wait_send()

    for n in range(1, 16):
        ok, copy = one(n)

        @pl.when(ok)
        def _():
            copy.wait_send()

    @pl.when(owner)
    def _():
        for n in range(1, 16):
            three(n).wait_send()
        for n in range(1, 8):
            two(n).wait_send()


def final_kernel(ret_ref, wf_ref, grad_ref, gc_ref, gwq_ref, gwk_ref, gwv_ref, gwo_ref):
    sort = by_feature()
    i, j = iotas((256, E))
    right = ones_where(i == j + 64)
    total = grad_ref[...].reshape(2 * ROWS, E).astype(F32)
    for half in range(2):
        parts = []
        for f in range(2):
            r = ret_ref[2 * f + half]
            parts += [r[:, 0:E], dot(r[:, 128:384], right).astype(BF)]
        total = total + t_dot(sort, jnp.concatenate(parts, 0))
    gc_ref[...] = total.astype(BF).reshape(ROWS, 2, E)

    i, j = iotas((384, E))

    def weight(first):
        low = ones_where((i == j + first) & (j < HALF))
        high = ones_where((i == j - HALF + first) & (j >= HALF))
        return dot(wf_ref[0], low) + dot(wf_ref[1], high)

    gwq_ref[...] = weight(0)
    gwo_ref[...] = weight(HALF).T
    gwk_ref[...] = weight(2 * HALF)
    gwv_ref[...] = weight(3 * HALF)


SLABS = 12
VM = pl.BlockSpec(memory_space=pltpu.VMEM)
DMA = pltpu.SemaphoreType.DMA


def sds(shape, dtype=BF):
    return jax.ShapeDtypeStruct(shape, dtype)


def share(*args):
    return pl.pallas_call(
        share_kernel,
        out_shape=[
            sds((NR // 2, 384)), sds((8, 128), F32), sds((2, 256, 256)), sds((2, 384, 384)), sds((128, NQ)), sds((128, NQ)),
            sds((384, PC)), sds((384, PC)),
        ],
        in_specs=[VM] * 2,
        out_specs=[VM] * 8,
        scratch_shapes=[
            pltpu.VMEM((PC, 384), BF), pltpu.VMEM((2, 2, 256, 128), BF),
            pltpu.VMEM((2, HALF, 384), BF), pltpu.VMEM((2, HALF, 384), BF),
            pltpu.VMEM((8, 128), F32), pltpu.VMEM((4, 8, 128), F32), pltpu.VMEM((2, 8, 128), F32), pltpu.VMEM((4, 8, 128), F32),
            DMA((4,)), DMA((4,)), DMA((4,)), DMA((4,)), DMA((8,)), DMA((8,)), DMA((4,)), DMA((4,)), DMA((16,)), DMA((16,)),
            DMA((4,)), DMA((4,)), DMA((4,)), DMA((4,)),
        ],
        compiler_params=pltpu.CompilerParams(collective_id=1, has_side_effects=True, vmem_limit_bytes=24 * 2**20),
        cost_estimate=pl.CostEstimate(flops=10**8, bytes_accessed=60 * 10**6, transcendentals=0),
        name="share",
    )(*args)


def attention(*args):
    return pl.pallas_call(
        attention_kernel,
        out_shape=[sds((NR // 2, 384)), sds((PC, 384), F32), sds((E, 384))],
        in_specs=[VM] * 8,
        out_specs=[VM] * 3,
        scratch_shapes=[
            pltpu.VMEM((NR, 3 * NQ), BF), pltpu.VMEM((BLOCKS, 8, 3 * NQ), F32), pltpu.VMEM((NR, 256), BF),
            pltpu.VMEM((3 * NQ, 128), BF), pltpu.VMEM((3 * NQ, 128), BF),
            pltpu.VMEM((128, 3 * NQ), BF), pltpu.VMEM((128, 3 * NQ), BF),
            pltpu.VMEM((48, 3 * NQ), F32), pltpu.VMEM((8, 3 * NQ), F32),
            pltpu.VMEM((2, PC, NQ), F32), pltpu.VMEM((KC, 256), BF),
            pltpu.VMEM((128, NQ), BF), pltpu.VMEM((128, NQ), BF), pltpu.VMEM((E, 256), F32),
        ],
        compiler_params=pltpu.CompilerParams(vmem_limit_bytes=VLIM * 2**20),
        cost_estimate=pl.CostEstimate(flops=3 * 10**10, bytes_accessed=10**7, transcendentals=14 * 10**6),
        name="attention",
    )(*args)


VLIM = 45


def reduce(*args):
    return pl.pallas_call(
        reduce_kernel,
        out_shape=[sds((4, HALF, 384)), sds((2, E, 384))],
        in_specs=[VM] * 3,
        out_specs=[VM] * 2,
        scratch_shapes=[
            pltpu.VMEM((4, PC, 384), BF), pltpu.VMEM((3, PC, 384), BF),
            pltpu.VMEM((192, 384), BF), pltpu.VMEM((192, 384), BF),
            pltpu.VMEM((PC, 384), BF), pltpu.VMEM((PC, 384), BF), pltpu.VMEM((PC, 384), BF),
            pltpu.VMEM((16, 16, 384), BF), pltpu.VMEM((8, 16, 384), BF),
            DMA((4,)), DMA((4,)), DMA((2,)), DMA((2,)), DMA((4,)), DMA((4,)), DMA((4,)), DMA((4,)),
            DMA((16,)), DMA((16,)), DMA((8,)), DMA((8,)), DMA((16,)), DMA((16,)),
        ],
        compiler_params=pltpu.CompilerParams(collective_id=2, has_side_effects=True, vmem_limit_bytes=24 * 2**20),
        cost_estimate=pl.CostEstimate(flops=10**8, bytes_accessed=60 * 10**6, transcendentals=0),
        name="reduce",
    )(*args)


def final(*args):
    w = sds((E, E), F32)
    return pl.pallas_call(
        final_kernel,
        out_shape=[sds((ROWS, 2, E)), w, w, w, w],
        in_specs=[VM] * 3,
        out_specs=[VM] * 5,
        compiler_params=pltpu.CompilerParams(vmem_limit_bytes=24 * 2**20),
        name="final",
    )(*args)


def body(cells, w_query, w_key, w_value, w_out, train_flag, grad_out):
    flags = jnp.broadcast_to(train_flag.astype(BF), (1, 2, ROWS))
    parts = share(jnp.concatenate([cells, grad_out, flags], 0), jnp.concatenate([w_query, w_key, w_value, w_out], 0))
    g, gq, w = attention(*parts)
    ret, wf = reduce(g, gq, w)
    return final(ret, wf, grad_out)


def solution(mesh):
    return jax.shard_map(
        body,
        mesh=mesh,
        in_specs=(P("row", "feat", None), P(), P(), P(), P(), P("row"), P("row", "feat", None)),
        out_specs=(P("row", "feat", None), P(), P(), P(), P()),
        check_vma=False,
    )
```

profile of v0, /device:TPU:25, one launch (start us, length us, event | category | flops | bytes accessed | tf_op | source)
XLA Modules:
  0.0 103.3 jit_solution(14205029193005191306)
XLA Ops:
  0.6 0.7 convert_element_type.3
  1.3 1.6 %pad_maximum_fusion.in_ref = bf16[385,2,192]{2,1,0:T(2,128)(2,1)S(1)} fusion(bf16[1,2,192]{2,1,0:T(2,128)(2,1)S(1)} %broadcast_in_dim.3, bf16[192,2,192]{2,1,0:T(2,128)(2,1)} %grad_ref.1, bf16[192,2,192]{2,1,0:T(2,128)(2,1)} %param.7), kind=kLoop, calls=%fused_computation | loop fusion | flops 295680 | bytes 591360 | tf_op jit(solution)/shard_map/concatenate | solution.py:704
  3.0 1.1 %pad_maximum_fusion.1.weights = bf16[768,192]{1,0:T(8,128)(2,1)S(1)} fusion(bf16[192,192]{1,0:T(8,128)(2,1)} %param.11, bf16[192,192]{1,0:T(8,128)(2,1)} %param.10, bf16[192,192]{1,0:T(8,128)(2,1)} %param.9, bf16[192,192]{1,0:T(8,128)(2,1)} %param.8), kind=kLoop, calls=%fused_computation.1 | loop fusion | flops 1179648 | bytes 589824 | tf_op jit(solution)/shard_map/concatenate | solution.py:704
  4.1 23.8 %share.1 = (bf16[3072,384]{1,0:T(8,128)(2,1)S(1)}, f32[8,128]{1,0:T(8,128)S(1)}, bf16[2,256,256]{2,1,0:T(8,128)(2,1)S(1)}, bf16[2,384,384]{2,1,0:T(8,128)(2,1)S(...) custom-call(bf16[385,2,192]{2,1,0:T(2,128)(2,1)S(1)} %pad_maximum_fu, ...), custom_call_target="tpu_custom_call" | custom-call | flops 100000000 | bytes 60000000 | tf_op jit(solution)/shard_map/share/pallas_call | solution.py:626
  27.9 45.9 %attention.1 = (bf16[3072,384]{1,0:T(8,128)(2,1)S(1)}, f32[384,384]{1,0:T(8,128)S(1)}, bf16[192,384]{1,0:T(8,128)(2,1)S(1)}) custom-call(bf16[3072,384]{1,0:T(8,128)(2,1)S(1)} %get-tuple-element.18.pk_ref, f32[8,128]{1,0:T(8,128)S(1)} %get-tuple-element.19.cnt_ref, bf16[2,256,256]{2,1,0:T(8,128)(2,1)S(1)} %get-tuple-element.20.wkv_ref, ...), custom_call_target="tpu_custom_call" | custom-call | flops 30000001024 | bytes 10000000 | tf_op jit(solution)/shard_map/attention/pallas_call | solution.py:648
  73.8 0.0 copy-start
  73.8 27.7 %reduce.1 = (bf16[4,96,384]{2,1,0:T(8,128)(2,1)S(1)}, bf16[2,192,384]{2,1,0:T(8,128)(2,1)S(1)}) custom-call(bf16[3072,384]{1,0:T(8,128)(2,1)S(1)} %get-tuple-element.26.g_ref, f32[384,384]{1,0:T(8,128)S(1)} %get-tuple-element.27.gq_ref, bf16[192,384]{1,0:T(8,128)(2,1)S(1)} %get-tuple-element.28.w_ref), custom_call_target="tpu_custom_call" | custom-call | flops 100000000 | bytes 60000000 | tf_op jit(solution)/shard_map/reduce/pallas_call | solution.py:671
  101.5 0.0 copy-done
  101.5 1.8 %final.1 = (bf16[192,2,192]{2,1,0:T(2,128)(2,1)}, f32[192,192]{1,0:T(8,128)}, f32[192,192]{1,0:T(8,128)}, f32[192,192]{1,0:T(8,128)}, f32[192,192]{1,0:T(8,128)}) custom-call(bf16[4,96,384]{2,1,0:T(8,128)(2,1)S(1)} %get-tuple-element.29.ret_ref, bf16[2,192,384]{2,1,0:T(8,128)(2,1)S(1)} %get-tuple-element.30.wf_ref, bf16[192,2,192]{2,1,0:T(2,128)(2,1)S(1)} %copy-done), custom_call_target="tpu_custom_call" | custom-call | tf_op jit(solution)/shard_map/final/pallas_call | solution.py:692
  (1 shorter events, 0.0 us)
Async XLA Ops:
  73.8 27.7 %copy-start = (bf16[192,2,192]{2,1,0:T(2,128)(2,1)S(1)}, bf16[192,2,192]{2,1,0:T(2,128)(2,1)}, u32[]{:S(2)}) copy-start(bf16[192,2,192]{2,1,0:T(2,128)(2,1)} %grad_ref.1) | copy-start | bytes 442372
where the time goes:
time: 105 us; the launch traced here: 103 us
  Pallas kernels  99.2 us (94%)
  other arithmetic  3.42 us (3%)
    pallas_call x1, Pallas kernels, attention(): pl.pallas_call(attention_kernel, out_shape=[sds((NR // 2, 384)), sds((PC,...  45.9 us
    pallas_call x1, Pallas kernels, reduce(): pl.pallas_call(reduce_kernel, out_shape=[sds((4, HALF, 384)), sds((2, E,...  27.7 us
    pallas_call x1, Pallas kernels, share(): pl.pallas_call(share_kernel, out_shape=[sds((NR // 2, 384)), sds((8, 128)...  23.8 us

commit v1 on v0

--- a/solution.py
+++ b/solution.py
@@ -249,7 +249,7 @@
             count(j).wait_send()
 
 
-def attention_kernel(pk_ref, cnt_ref, wkv_ref, u_ref, qT_ref, gT_ref, poT_ref, goT_ref, g_ref, gq_ref, w_ref, e_ref, mb_ref, kv_ref, qm_ref, gm_ref,
+def attention_kernel(pk_ref, cnt_ref, wkv_ref, u_ref, qT_ref, gT_ref, poT_ref, goT_ref, g_ref, dq_ref, w_ref, e_ref, mb_ref, kv_ref, qm_ref, gm_ref,
                      qmT_ref, gmT_ref, acc_ref, m_ref, s_ref, dkv_ref, attT_ref, dqT_ref, wacc_ref):
     train = jnp.max(cnt_ref[...]).astype(jnp.int32)
     halves = lax.div(train + PC - 1, PC)
@@ -396,7 +396,7 @@
         dqT_ref[hs, :] = (acc_ref[0:32, q] * SCALE).astype(BF)
 
     dq, at = dqT_ref[...].T, attT_ref[...].T
-    gq_ref[...] = dot(dq[0:PC], u_ref[0, 256:384, :]) + dot(dq[PC:NQ], u_ref[1, 256:384, :])
+    dq_ref[...] = dq
     poT, goT = poT_ref[...], goT_ref[...]
     w_q = dot(poT[0:E], dq[0:PC]) + dot(poT[E:2 * E], dq[PC:NQ])
     w_o = dot(goT[0:E], at[0:PC]) + dot(goT[E:2 * E], at[PC:NQ])
@@ -408,7 +408,7 @@
     ).astype(BF)
 
 
-def reduce_kernel(g_ref, gq_ref, w_ref, ret_ref, wf_ref,
+def reduce_kernel(g_ref, dq_ref, u_ref, w_ref, ret_ref, wf_ref,
                   tw, part, hp, hn, fp, fn, fin, rs, p2,
                   ts, tr, hs_, hr, fs, fr, ks, kr, as_, ar, bs, br, cs, cr):
     z, x, yl, yh, c = place()
@@ -532,7 +532,7 @@
         for n in range(1, 16):
             three(n).start()
 
-    total = with_twin(3, z) + gq_ref[...]
+    total = with_twin(3, z) + dot(dq_ref[0:PC, :], u_ref[0, 256:384, :]) + dot(dq_ref[PC:NQ, :], u_ref[1, 256:384, :])
     wait_for(fp.at[hi, :], fr.at[0])
     wait_for(fn.at[lo, :], fr.at[1])
     wait_for(fp.at[lo, :], fr.at[2])
@@ -647,7 +647,7 @@
 def attention(*args):
     return pl.pallas_call(
         attention_kernel,
-        out_shape=[sds((NR // 2, 384)), sds((PC, 384), F32), sds((E, 384))],
+        out_shape=[sds((NR // 2, 384)), sds((NQ, 128)), sds((E, 384))],
         in_specs=[VM] * 8,
         out_specs=[VM] * 3,
         scratch_shapes=[
@@ -671,7 +671,7 @@
     return pl.pallas_call(
         reduce_kernel,
         out_shape=[sds((4, HALF, 384)), sds((2, E, 384))],
-        in_specs=[VM] * 3,
+        in_specs=[VM] * 4,
         out_specs=[VM] * 2,
         scratch_shapes=[
             pltpu.VMEM((4, PC, 384), BF), pltpu.VMEM((3, PC, 384), BF),
@@ -702,8 +702,8 @@
 def body(cells, w_query, w_key, w_value, w_out, train_flag, grad_out):
     flags = jnp.broadcast_to(train_flag.astype(BF), (1, 2, ROWS))
     parts = share(jnp.concatenate([cells, grad_out, flags], 0), jnp.concatenate([w_query, w_key, w_value, w_out], 0))
-    g, gq, w = attention(*parts)
-    ret, wf = reduce(g, gq, w)
+    g, dq, w = attention(*parts)
+    ret, wf = reduce(g, dq, parts[3], w)
     return final(ret, wf, grad_out)
 
 

time: 105 us -> 87.4 us (0.83); the launches traced: 103 us -> 88.6 us
  Pallas kernels: 99.2 us -> 84.5 us
    pallas_call x1, Pallas kernels: 45.9 us -> 31.1 us  [attention(): pl.pallas_call(attention_kernel, out_shape=[sds((NR // 2, 384)), sds((NQ,...]
where the time goes in v1:
time: 87.4 us; the launch traced here: 88.6 us
  Pallas kernels  84.5 us (97%)
  other arithmetic  3.42 us (4%)
    pallas_call x1, Pallas kernels, attention(): pl.pallas_call(attention_kernel, out_shape=[sds((NR // 2, 384)), sds((NQ,...  31.1 us
    pallas_call x1, Pallas kernels, reduce(): pl.pallas_call(reduce_kernel, out_shape=[sds((4, HALF, 384)), sds((2, E,...  27.7 us
    pallas_call x1, Pallas kernels, share(): pl.pallas_call(share_kernel, out_shape=[sds((NR // 2, 384)), sds((8, 128)...  23.8 us
    pallas_call x1, Pallas kernels, final(): pl.pallas_call(final_kernel, out_shape=[sds((ROWS, 2, E)), w, w, w, w], i...  1.83 us

profile of v1, /device:TPU:25, one launch (start us, length us, event | category | flops | bytes accessed | tf_op | source)
XLA Modules:
  0.0 88.6 jit_solution(5023111841981074921)
XLA Ops:
  0.6 0.7 convert_element_type.3
  1.3 1.6 %pad_maximum_fusion.in_ref = bf16[385,2,192]{2,1,0:T(2,128)(2,1)S(1)} fusion(bf16[1,2,192]{2,1,0:T(2,128)(2,1)S(1)} %broadcast_in_dim.3, bf16[192,2,192]{2,1,0:T(2,128)(2,1)} %grad_ref.1, bf16[192,2,192]{2,1,0:T(2,128)(2,1)} %param.7), kind=kLoop, calls=%fused_computation | loop fusion | flops 295680 | bytes 591360 | tf_op jit(solution)/shard_map/concatenate | solution.py:704
  3.0 1.1 %pad_maximum_fusion.1.weights = bf16[768,192]{1,0:T(8,128)(2,1)S(1)} fusion(bf16[192,192]{1,0:T(8,128)(2,1)} %param.11, bf16[192,192]{1,0:T(8,128)(2,1)} %param.10, bf16[192,192]{1,0:T(8,128)(2,1)} %param.9, bf16[192,192]{1,0:T(8,128)(2,1)} %param.8), kind=kLoop, calls=%fused_computation.1 | loop fusion | flops 1179648 | bytes 589824 | tf_op jit(solution)/shard_map/concatenate | solution.py:704
  4.1 23.8 %share.1 = (bf16[3072,384]{1,0:T(8,128)(2,1)S(1)}, f32[8,128]{1,0:T(8,128)S(1)}, bf16[2,256,256]{2,1,0:T(8,128)(2,1)S(1)}, bf16[2,384,384]{2,1,0:T(8,128)(2,1)S(...) custom-call(bf16[385,2,192]{2,1,0:T(2,128)(2,1)S(1)} %pad_maximum_fu, ...), custom_call_target="tpu_custom_call" | custom-call | flops 100000000 | bytes 60000000 | tf_op jit(solution)/shard_map/share/pallas_call | solution.py:626
  27.9 31.1 %attention.1 = (bf16[3072,384]{1,0:T(8,128)(2,1)S(1)}, bf16[768,128]{1,0:T(8,128)(2,1)S(1)}, bf16[192,384]{1,0:T(8,128)(2,1)S(1)}) custom-call(bf16[3072,384]{1,0:T(8,128)(2,1)S(1)} %get-tuple-element.18.pk_ref, f32[8,128]{1,0:T(8,128)S(1)} %get-tuple-element.19.cnt_ref, bf16[2,256,256]{2,1,0:T(8,128)(2,1)S(1)} %get-tuple-element.20.wkv_ref, ...), custom_call_target="tpu_custom_call" | custom-call | flops 30000001024 | bytes 10000000 | tf_op jit(solution)/shard_map/attention/pallas_call | solution.py:648
  59.0 0.0 copy-start
  59.0 27.7 %reduce.1 = (bf16[4,96,384]{2,1,0:T(8,128)(2,1)S(1)}, bf16[2,192,384]{2,1,0:T(8,128)(2,1)S(1)}) custom-call(bf16[3072,384]{1,0:T(8,128)(2,1)S(1)} %get-tuple-element.26.g_ref, bf16[768,128]{1,0:T(8,128)(2,1)S(1)} %get-tuple-element.27.dq_ref, bf16[2,384,384]{2,1,0:T(8,128)(2,1)S(1)} %get-tuple-element.21.u_ref, bf16[192,384]{1,0:T(8,128)(2,1)S(1)} %get-tuple-element.28.w_ref), custom_call_target="tpu_custom_call" | custom-call | flops 100000000 | bytes 60000000 | tf_op jit(solution)/shard_map/reduce/pallas_call | solution.py:671
  86.7 0.0 copy-done
  86.7 1.8 %final.1 = (bf16[192,2,192]{2,1,0:T(2,128)(2,1)}, f32[192,192]{1,0:T(8,128)}, f32[192,192]{1,0:T(8,128)}, f32[192,192]{1,0:T(8,128)}, f32[192,192]{1,0:T(8,128)}) custom-call(bf16[4,96,384]{2,1,0:T(8,128)(2,1)S(1)} %get-tuple-element.29.ret_ref, bf16[2,192,384]{2,1,0:T(8,128)(2,1)S(1)} %get-tuple-element.30.wf_ref, bf16[192,2,192]{2,1,0:T(2,128)(2,1)S(1)} %copy-done), custom_call_target="tpu_custom_call" | custom-call | tf_op jit(solution)/shard_map/final/pallas_call | solution.py:692
  (1 shorter events, 0.0 us)
Async XLA Ops:
  59.0 27.7 %copy-start = (bf16[192,2,192]{2,1,0:T(2,128)(2,1)S(1)}, bf16[192,2,192]{2,1,0:T(2,128)(2,1)}, u32[]{:S(2)}) copy-start(bf16[192,2,192]{2,1,0:T(2,128)(2,1)} %grad_ref.1) | copy-start | bytes 442372
